TPU v7x, 32 devices: a whole 2x2x4 slice. The times are simulated.
32 devices in a mesh: gx: 8 (over z, y), gz: 4 (over x, core).
Axes of the slice: x: 2, y: 2, z: 4, core: 2. Of those that a mesh axis runs over, the one named last changes fastest.
Arguments:
- whitened: float32 [2, 64, 1024, 512], P(None, 'gz', 'gx'), may hold values from -6 to 6
- observed: float32 [2, 1024, 512], P(None, 'gx'), may hold values from -12 to 12
- lower_x: bfloat16 [1024, 1024], P('gx'), as said below
- lower_y: bfloat16 [512, 512], P('gx'), as said below
- lower_z: bfloat16 [64, 64], replicated, as said below
- coupling_kernel: float32 [2, 3, 3, 3], replicated, may hold values from -1.25 to 1.25
Outputs:
- gradient: float32 [2, 64, 1024, 512], P(None, 'gz', 'gx')
- misfit: float32 [2, 1024, 512], P(None, 'gx')
Inputs may be any that keep to these rules, and one draw needn't show every extreme that they name: `lower_x`: lower triangular: zero above the diagonal, diagonal entries between 0.5 and 1.5. `lower_y`: lower triangular: zero above the diagonal, diagonal entries between 0.5 and 1.5. `lower_z`: lower triangular: zero above the diagonal, diagonal entries between 0.5 and 1.5.
All inputs are finite; a program needn't handle non-finite values.
Results may differ from a plain program's by a relative error of at most 0.013.
The roundings to bfloat16 on the way count: a program that leaves them out, or rounds other values in their place, can miss the bound.
Values may be sent and summed in bfloat16 or wider, within the bound.
A program may use at most 128 MiB of HBM per device.

v0:
```python
import math
import jax
import jax.numpy as jnp
from jax import lax
from jax.sharding import PartitionSpec as P

NZ = 64


def padded_2(x, sides, width):
    for axis, dim in sides:
        peers, length = (lax.axis_size(axis), x.shape[dim])
        up = [(i, (i + 1) % peers) for i in range(peers - 1)]
        down = [(j, i) for i, j in up]
        last = lax.slice_in_dim(x, length - width, length, axis=dim)
        first = lax.slice_in_dim(x, 0, width, axis=dim)
        before = lax.ppermute(last, axis, up)
        after = lax.ppermute(first, axis, down)
        x = jnp.concatenate([before, x, after], axis=dim)
    return x


def depth_lines(values, local_step):
    turned = lax.all_to_all(values, "gz", split_axis=3, concat_axis=1, tiled=True)
    return lax.all_to_all(local_step(turned), "gz", split_axis=1, concat_axis=3, tiled=True)


def across_lines(values, local_step):
    turned = lax.all_to_all(values, "gx", split_axis=3, concat_axis=2, tiled=True)
    return lax.all_to_all(local_step(turned), "gx", split_axis=2, concat_axis=3, tiled=True)


def stencil_sum(padded, kernel, depth_rows, x_rows, y_rows, flipped):
    total = jnp.zeros(padded.shape[:-3] + (depth_rows, x_rows, y_rows), jnp.float32)
    for offset_z in range(3):
        for offset_x in range(3):
            for offset_y in range(3):
                start_z = 2 - offset_z if flipped else offset_z
                start_x = 2 - offset_x if flipped else offset_x
                start_y = 2 - offset_y if flipped else offset_y
                total = (
                    total
                    + kernel[offset_z, offset_x, offset_y]
                    * padded[
                        ...,
                        start_z : start_z + depth_rows,
                        start_x : start_x + x_rows,
                        start_y : start_y + y_rows,
                    ]
                )
    return total


def depth_weights(first_row, depth_rows):
    depth = (first_row + jnp.arange(depth_rows)).astype(jnp.float32)
    factor = 4.0 / math.sqrt(NZ)
    return (factor / (1.0 + depth / NZ) ** 2, factor / (1.0 + depth / NZ) ** 3)


def coupling_forward(rim, magnetic_f, kernel, shape):
    depth_rows, x_rows, y_rows = shape
    pre_scale = stencil_sum(rim, kernel[0], depth_rows, x_rows, y_rows, False)
    pre_shift = stencil_sum(rim, kernel[1], depth_rows, x_rows, y_rows, False)
    scale = jnp.tanh(pre_scale)
    growth = jnp.exp(scale)
    return (scale, growth, magnetic_f * growth + pre_shift)


def local(whitened, observed, lower_x, lower_y, lower_z, coupling_kernel):
    factor_x, factor_y = (
        lax.all_gather(lower_x, "gx", axis=0, tiled=True),
        lax.all_gather(lower_y, "gx", axis=0, tiled=True),
    )

    def apply_depth(values):
        return jnp.einsum(
            "zk,fkxy->fzxy", lower_z, values, preferred_element_type=jnp.float32
        ).astype(jnp.bfloat16)

    def apply_across(values):
        return jnp.einsum(
            "xk,fzky->fzxy", factor_x, values, preferred_element_type=jnp.float32
        ).astype(jnp.bfloat16)

    def depth_adjoint(values):
        return jnp.einsum(
            "kz,fkxy->fzxy", lower_z, values, preferred_element_type=jnp.float32
        ).astype(jnp.bfloat16)

    def across_adjoint(values):
        return jnp.einsum(
            "kx,fzky->fzxy", factor_x, values, preferred_element_type=jnp.float32
        ).astype(jnp.bfloat16)

    start = whitened.astype(jnp.bfloat16)
    first = jnp.einsum("fzxk,yk->fzxy", start, factor_y, preferred_element_type=jnp.float32).astype(
        jnp.bfloat16
    )
    model = across_lines(depth_lines(first, apply_depth), apply_across)
    density = model[0]
    magnetic_f = model[1].astype(jnp.float32)
    depth_rows, x_rows, y_rows = density.shape
    rim = padded_2(density, (("gx", 1), ("gz", 0)), 1)
    rim = jnp.pad(rim, ((0, 0), (0, 0), (1, 1))).astype(jnp.float32)
    scale, growth, coupled = coupling_forward(
        rim, magnetic_f, coupling_kernel, (depth_rows, x_rows, y_rows)
    )
    weight_g, weight_m = depth_weights(lax.axis_index("gz") * depth_rows, depth_rows)
    part_g = jnp.einsum("z,zxy->xy", weight_g, density.astype(jnp.float32))
    part_m = jnp.einsum("z,zxy->xy", weight_m, coupled)
    predicted = lax.psum(jnp.stack([part_g, part_m]), "gz")
    misfit = predicted - observed
    back_g = weight_g[:, None, None] * misfit[0][None]
    back_m = weight_m[:, None, None] * misfit[1][None]
    back_scale = (back_m * magnetic_f * growth * (1.0 - scale * scale)).astype(jnp.bfloat16)
    back_shift = back_m.astype(jnp.bfloat16)
    cotangents = jnp.stack([back_scale, back_shift])
    outer = padded_2(cotangents, (("gx", 2), ("gz", 1)), 1)
    outer = jnp.pad(outer, ((0, 0), (0, 0), (0, 0), (1, 1))).astype(jnp.float32)
    spread_back = stencil_sum(outer[0], coupling_kernel[0], depth_rows, x_rows, y_rows, True)
    spread_back = spread_back + stencil_sum(
        outer[1], coupling_kernel[1], depth_rows, x_rows, y_rows, True
    )
    adjoint = jnp.stack([back_g + spread_back, back_m * growth]).astype(jnp.bfloat16)
    fourth = depth_lines(across_lines(adjoint, across_adjoint), depth_adjoint)
    gradient = whitened + jnp.einsum(
        "fzxk,ky->fzxy", fourth, factor_y, preferred_element_type=jnp.float32
    )
    return (gradient, misfit)


def solution(mesh):
    in_specs = (
        P(None, "gz", "gx", None),
        P(None, "gx", None),
        P("gx", None),
        P("gx", None),
        P(),
        P(),
    )
    out_specs = (P(None, "gz", "gx", None), P(None, "gx", None))
    return jax.shard_map(local, mesh=mesh, in_specs=in_specs, out_specs=out_specs, check_vma=False)
```

profile of v0, /device:TPU:0, one launch (start us, length us, event | category | flops | bytes accessed | tf_op | source)
XLA Modules:
  0.0 1367.9 jit_solution(581240853023325873)
XLA Ops:
  7.2 33.2 %all_gather.6 = bf16[512,512]{1,0:T(8,128)(2,1)S(1)} all-gather(bf16[64,512]{1,0:T(8,128)(2,1)} %param.9), channel_id=1, replica_groups=mesh['gx'=8,'gz'=4] {'gx'}, dimensions={0}, use_global_device_ids=true | all-gather | bytes 589824 | tf_op jit(solution)/shard_map/all_gather | solution.py:72
  56.9 53.9 %all_to_all.141 = bf16[2,16,128,512]{2,1,0,3:T(8,128)(2,1)} all-to-all(bf16[2,16,128,512]{2,1,0,3:T(8,128)(2,1)} %copy.51), channel_id=1, replica_groups=mesh['gx'=8,'gz'=4] {'gz'}, dimensions={3} | all-to-all | bytes 8388608 | tf_op jit(solution)/shard_map/all_to_all | solution.py:24
  125.8 51.6 %all_to_all.142 = bf16[2,64,128,128]{3,2,0,1:T(8,128)(2,1)} all-to-all(bf16[2,64,128,128]{3,2,0,1:T(8,128)(2,1)S(1)} %copy.53), channel_id=1, replica_groups=mesh['gx'=8,'gz'=4] {'gz'}, dimensions={1} | all-to-all | bytes 8388608 | tf_op jit(solution)/shard_map/all_to_all | solution.py:25
  191.7 117.5 %all-to-all-done.2 = bf16[2,16,128,512]{2,1,0,3:T(8,128)(2,1)} async-done(((bf16[2,16,128,512]{2,1,0,3:T(8,128)(2,1)}), bf16[2,16,128,512]{2,1,0,3:T(8,128)(2,1)}, u32[]{:S(2)}, u32[]{:S(2)}) %all-to-all-start.2) | async-done | bytes 4194336 | tf_op jit(solution)/shard_map/all_to_all | solution.py:29
  323.4 9.5 convert_bitcast_fusion.2
  332.8 12.9 copy.59
  345.7 10.5 reshape.38
  363.3 90.1 %all-to-all-done.3 = bf16[8,2,131072]{2,1,0:T(2,128)(2,1)} async-done(((bf16[8,2,131072]{2,1,0:T(2,128)(2,1)}), bf16[8,2,131072]{2,1,0:T(2,128)(2,1)}, u32[]{:S(2)}, u32[]{:S(2)}) %all-to-all-start.3) | async-done | bytes 4194336 | tf_op jit(solution)/shard_map/all_to_all | solution.py:30
  453.4 10.3 reshape.39
  463.7 9.3 copy.97
  506.6 11.2 fusion.10
  517.8 122.0 %add_add_fusion = (bf16[16,128,512]{1,2,0:T(8,128)(2,1)S(1)}, f32[16,128,512]{1,2,0:T(8,128)}) fusion(f32[16,128,512]{1,2,0:T(8,128)} %bitcast.166, f32[18,130,514]{1,2,0:T(8,128)} %fusion.10, f32[]{:T(128)} %bitcast.79, f32[]{:T(128)} %bitcast.78, f32[]{:T(128)} %bitcast.77, f32[]{:T(128)} %bitcast.76, f32[]{:T(128)} %bitcast.75, f32[]{:T(128)} %bitcast.74, ...), kind=kLoop, calls=%fused_computation.148 | loop fusion | flops 114294784 | bytes 123732184 | tf_op jit(solution)/shard_map/add | solution.py:66
  645.7 35.0 %all-reduce.4.cloned.1.call-done = f32[2,128,512]{2,1,0:T(8,128)} async-done(((f32[2,128,512]{2,1,0:T(8,128)}), f32[2,128,512]{2,1,0:T(8,128)}) %all-reduce.4.cloned.1.call-update) | async-done | bytes 524304 | tf_op jit(solution)/shard_map/psum | solution.py:111
  723.4 22.6 %fusion.1 = f32[2,18,130,514]{2,3,1,0:T(8,128)S(1)} fusion(bf16[2,1,130,512]{2,3,1,0:T(8,128)(2,1)} %collective-permute-done.7, bf16[2,1,130,512]{2,3,1,0:T(8,128)(2,1)S(1)} %collective-permute-done.6, bf16[2,16,1,512]{2,3,1,0:T(8,128)(2,1)} %copy.73, bf16[2,16,1,512]{2,3,1,0:T(8,128)(2,1)} %copy.72, bf16[1,16,128,512]{2,3,1,0:T(8,128)(2,1)S(1)} %multiply_convert_fusion, ...), kind=kLoop, calls=%fused_computation.8 | loop fusion | flops 50515920 | bytes 14414400 | tf_op jit(solution)/shard_map/convert_element_type | solution.py:119
  752.9 196.9 %fusion.84 = bf16[1,16,128,512]{2,3,1,0:T(8,128)(2,1)S(1)} fusion(f32[18,130,514]{1,2,0:T(8,128)} %get-tuple-element.5, f32[]{:T(128)} %bitcast.79, f32[]{:T(128)} %bitcast.78, f32[]{:T(128)} %bitcast.77, f32[]{:T(128)} %bitcast.76, f32[]{:T(128)} %bitcast.75, f32[]{:T(128)} %bitcast.74, f32[]{:T(128)} %bitcast.73, f32[]{:T(128)} %bitcast.72, f32[]{:T(128)} %bitcast.71, ...), kind=kLoop, calls=%fused_computation.161 | loop fusion | flops 115343360 | bytes 228852000 | tf_op jit(solution)/shard_map/stack | solution.py:124
  952.9 97.5 %all_to_all.143 = bf16[2,16,128,512]{2,1,0,3:T(8,128)(2,1)S(1)} all-to-all(bf16[2,16,128,512]{2,1,0,3:T(8,128)(2,1)S(1)} %copy.74), channel_id=1, replica_groups=mesh['gx'=8,'gz'=4] {'gx'}, dimensions={3} | all-to-all | bytes 8388608 | tf_op jit(solution)/shard_map/all_to_all | solution.py:29
  1071.0 12.9 copy.77
  1083.9 10.5 reshape.40
  1094.3 97.9 %all_to_all.144 = bf16[8,2,131072]{2,1,0:T(2,128)(2,1)} all-to-all(bf16[8,2,131072]{2,1,0:T(2,128)(2,1)} %reshape.40), channel_id=1, replica_groups=mesh['gx'=8,'gz'=4] {'gx'}, dimensions={0} | all-to-all | bytes 8388608 | tf_op jit(solution)/shard_map/all_to_all | solution.py:30
  1192.2 10.3 reshape.41
  1202.5 14.8 %copy.101 = bf16[2,16,128,8,64]{2,1,0,4,3:T(8,128)(2,1)} copy(bf16[2,16,128,8,64]{4,1,0,2,3:T(8,128)(2,1)} %bitcast.171) | data formatting | bytes 8388608 | tf_op jit(solution)/shard_map/all_to_all | solution.py:30
  1217.2 54.1 %all_to_all.145 = bf16[2,16,128,512]{2,1,0,3:T(8,128)(2,1)} all-to-all(bf16[2,16,128,512]{2,1,0,3:T(8,128)(2,1)} %bitcast.173), channel_id=1, replica_groups=mesh['gx'=8,'gz'=4] {'gz'}, dimensions={3} | all-to-all | bytes 8388608 | tf_op jit(solution)/shard_map/all_to_all | solution.py:24
  1286.5 50.7 %all_to_all.146 = bf16[2,64,128,128]{3,2,0,1:T(8,128)(2,1)S(1)} all-to-all(bf16[2,64,128,128]{3,2,0,1:T(8,128)(2,1)S(1)} %copy.84), channel_id=1, replica_groups=mesh['gx'=8,'gz'=4] {'gz'}, dimensions={1} | all-to-all | bytes 8388608 | tf_op jit(solution)/shard_map/all_to_all | solution.py:25
  1350.4 10.4 convolution_add_fusion
  (103 shorter events, 207.8 us)
Async XLA Ops:
  7.2 112.5 %copy-start = (bf16[64,64]{1,0:T(8,128)(2,1)S(1)}, bf16[64,64]{1,0:T(8,128)(2,1)}, u32[]{:S(2)}) copy-start(bf16[64,64]{1,0:T(8,128)(2,1)} %param.10) | copy-start | bytes 24580
  40.4 0.8 copy-start.7
  185.3 123.9 %all-to-all-start.2 = ((bf16[2,16,128,512]{2,1,0,3:T(8,128)(2,1)}), bf16[2,16,128,512]{2,1,0,3:T(8,128)(2,1)}, u32[]{:S(2)}, u32[]{:S(2)}) async-start(bf16[2,16,128,512]{2,1,0,3:T(8,128)(2,1)} %bitcast.174), calls=%async_computation.2 | async-start | bytes 8388608 | tf_op jit(solution)/shard_map/all_to_all | solution.py:29
  191.0 132.4 %all-gather.2.cloned.1.call-start = ((), (), s32[]{:S(2)}) async-start(), calls=%async_computation.8 | async-start | bytes 2359296 | tf_op jit(solution)/shard_map/all_gather | solution.py:71
  356.2 4.9 copy-start.11
  356.2 97.2 %all-to-all-start.3 = ((bf16[8,2,131072]{2,1,0:T(2,128)(2,1)}), bf16[8,2,131072]{2,1,0:T(2,128)(2,1)}, u32[]{:S(2)}, u32[]{:S(2)}) async-start(bf16[8,2,131072]{2,1,0:T(2,128)(2,1)} %reshape.38), calls=%async_computation.3 | async-start | bytes 8388608 | tf_op jit(solution)/shard_map/all_to_all | solution.py:30
  360.9 319.8 %all-reduce.4.cloned.1.call-start = ((), (), s32[]{:S(2)}) async-start(), calls=%async_computation.9 | async-start | bytes 1048576 | tf_op jit(solution)/shard_map/psum | solution.py:111
  485.1 11.4 collective-permute-start.1
  486.4 8.3 collective-permute-start
  498.3 4.3 copy-start.5
  498.3 4.8 copy-start.4
  499.9 6.0 collective-permute-start.2
  501.4 4.6 collective-permute-start.3
  503.1 2.8 copy-start.2
  503.2 3.4 copy-start.3
  639.8 41.0 %copy-start.10 = (f32[2,128,512]{2,1,0:T(8,128)S(1)}, f32[2,128,512]{2,1,0:T(8,128)}, u32[]{:S(2)}) copy-start(f32[2,128,512]{2,1,0:T(8,128)} %param.7) | copy-start | bytes 1572868
  689.7 4.5 copy-start.1
  697.9 8.7 collective-permute-start.4
  705.3 5.8 collective-permute-start.5
  717.2 3.0 collective-permute-start.6
  718.5 4.9 collective-permute-start.7
  752.9 196.9 %copy-start.6 = (bf16[1,16,128,512]{2,3,1,0:T(8,128)(2,1)S(1)}, bf16[1,16,128,512]{2,3,1,0:T(8,128)(2,1)}, u32[]{:S(2)}) copy-start(bf16[1,16,128,512]{2,3,1,0:T(8,128)(2,1)} %get-tuple-element.11) | copy-start | bytes 6291460
  1055.1 7.4 copy-start.12
  1343.1 7.3 copy-start.8
  (1 other events, 0.8 us)
Sparse Core Ops, SparseCore 0:
  193.9 102.6 all-gather.1
  645.8 34.8 all-reduce.3
where the time goes:
time: 1380 us; the launch traced here: 1370 us
  blocking collectives  439 us (32%)
  other arithmetic  376 us (27%)
  waiting for transfers between devices  248 us (18%)
  local copies, waits for them, and re-layouts  219 us (16%)
  matrix products  45.4 us (3%)
  starting transfers between devices  26.9 us (2%)
  between operations  14.6 us (1%)
    another operation x2, other arithmetic, local(): jnp.stack([back_g + spread_back, back_m * growth]).astype(jnp.bfloat16)  197 us
    add x1, other arithmetic, coupling_forward(): return (scale, growth, magnetic_f * growth + pre_shift)  122 us
    all_to_all x1, waiting for transfers between devices, across_lines(): lax.all_to_all(values, 'gx', split_axis=3, concat_axis=2, tiled=True)  117 us
    all_to_all x2, blocking collectives, depth_lines(): lax.all_to_all(values, 'gz', split_axis=3, concat_axis=1, tiled=True)  108 us
    all_to_all x2, blocking collectives, depth_lines(): lax.all_to_all(local_step(turned), 'gz', split_axis=1, concat_axis=3, til...  102 us
    all_to_all x1, blocking collectives, across_lines(): lax.all_to_all(local_step(turned), 'gx', split_axis=2, concat_axis=3, til...  97.9 us
    all_to_all x1, blocking collectives, across_lines(): lax.all_to_all(values, 'gx', split_axis=3, concat_axis=2, tiled=True)  97.5 us
    all_to_all x1, waiting for transfers between devices, across_lines(): lax.all_to_all(local_step(turned), 'gx', split_axis=2, concat_axis=3, til...  90.1 us
  transfers between devices with their start and end apart: 12, of which 6 were waited for; matrix products, arithmetic and copies ran while one was open for 2% of the time, Pallas kernels for 0%

commit v1 on v0

--- a/solution.py
+++ b/solution.py
@@ -108,7 +108,7 @@
     weight_g, weight_m = depth_weights(lax.axis_index("gz") * depth_rows, depth_rows)
     part_g = jnp.einsum("z,zxy->xy", weight_g, density.astype(jnp.float32))
     part_m = jnp.einsum("z,zxy->xy", weight_m, coupled)
-    predicted = lax.psum(jnp.stack([part_g, part_m]), "gz")
+    predicted = jnp.sum(lax.all_gather(jnp.stack([part_g, part_m]), "gz"), axis=0)
     misfit = predicted - observed
     back_g = weight_g[:, None, None] * misfit[0][None]
     back_m = weight_m[:, None, None] * misfit[1][None]

time: 1380 us -> 1370 us (level)
    psum x1 -> x0, waiting for transfers between devices: 35 us -> none  [local(): predicted = lax.psum(jnp.stack([part_g, part_m]), 'gz')]
    all_gather x0 -> x1, waiting for transfers between devices: none -> 24.5 us  [local(): lax.all_gather(jnp.stack([part_g, part_m]), 'gz')]
where the time goes in v1:
time: 1370 us; the launch traced here: 1360 us
  blocking collectives  439 us (32%)
  other arithmetic  377 us (28%)
  waiting for transfers between devices  237 us (17%)
  local copies, waits for them, and re-layouts  218 us (16%)
  matrix products  45.4 us (3%)
  starting transfers between devices  27.3 us (2%)
  between operations  14.6 us (1%)
    another operation x2, other arithmetic, local(): jnp.stack([back_g + spread_back, back_m * growth]).astype(jnp.bfloat16)  197 us
    add x1, other arithmetic, coupling_forward(): return (scale, growth, magnetic_f * growth + pre_shift)  122 us
    all_to_all x1, waiting for transfers between devices, across_lines(): lax.all_to_all(values, 'gx', split_axis=3, concat_axis=2, tiled=True)  117 us
    all_to_all x2, blocking collectives, depth_lines(): lax.all_to_all(values, 'gz', split_axis=3, concat_axis=1, tiled=True)  108 us
    all_to_all x2, blocking collectives, depth_lines(): lax.all_to_all(local_step(turned), 'gz', split_axis=1, concat_axis=3, til...  102 us
    all_to_all x1, blocking collectives, across_lines(): lax.all_to_all(local_step(turned), 'gx', split_axis=2, concat_axis=3, til...  97.9 us
    all_to_all x1, blocking collectives, across_lines(): lax.all_to_all(values, 'gx', split_axis=3, concat_axis=2, tiled=True)  97.5 us
    all_to_all x1, waiting for transfers between devices, across_lines(): lax.all_to_all(local_step(turned), 'gx', split_axis=2, concat_axis=3, til...  90.1 us
  transfers between devices with their start and end apart: 12, of which 6 were waited for; matrix products, arithmetic and copies ran while one was open for 2% of the time, Pallas kernels for 0%

profile of v1, /device:TPU:0, one launch (start us, length us, event | category | flops | bytes accessed | tf_op | source)
XLA Modules:
  0.0 1358.2 jit_solution(16255518293962539466)
XLA Ops:
  7.2 33.2 %all_gather.12 = bf16[512,512]{1,0:T(8,128)(2,1)S(1)} all-gather(bf16[64,512]{1,0:T(8,128)(2,1)} %param.9), channel_id=1, replica_groups=mesh['gx'=8,'gz'=4] {'gx'}, dimensions={0}, use_global_device_ids=true | all-gather | bytes 589824 | tf_op jit(solution)/shard_map/all_gather | solution.py:72
  56.9 53.9 %all_to_all.141 = bf16[2,16,128,512]{2,1,0,3:T(8,128)(2,1)} all-to-all(bf16[2,16,128,512]{2,1,0,3:T(8,128)(2,1)} %copy.51), channel_id=1, replica_groups=mesh['gx'=8,'gz'=4] {'gz'}, dimensions={3} | all-to-all | bytes 8388608 | tf_op jit(solution)/shard_map/all_to_all | solution.py:24
  125.8 51.6 %all_to_all.142 = bf16[2,64,128,128]{3,2,0,1:T(8,128)(2,1)} all-to-all(bf16[2,64,128,128]{3,2,0,1:T(8,128)(2,1)S(1)} %copy.53), channel_id=1, replica_groups=mesh['gx'=8,'gz'=4] {'gz'}, dimensions={1} | all-to-all | bytes 8388608 | tf_op jit(solution)/shard_map/all_to_all | solution.py:25
  191.7 117.5 %all-to-all-done.2 = bf16[2,16,128,512]{2,1,0,3:T(8,128)(2,1)} async-done(((bf16[2,16,128,512]{2,1,0,3:T(8,128)(2,1)}), bf16[2,16,128,512]{2,1,0,3:T(8,128)(2,1)}, u32[]{:S(2)}, u32[]{:S(2)}) %all-to-all-start.2) | async-done | bytes 4194336 | tf_op jit(solution)/shard_map/all_to_all | solution.py:29
  323.4 9.5 convert_bitcast_fusion.2
  332.8 12.9 copy.59
  345.7 10.5 reshape.39
  363.3 90.1 %all-to-all-done.3 = bf16[8,2,131072]{2,1,0:T(2,128)(2,1)} async-done(((bf16[8,2,131072]{2,1,0:T(2,128)(2,1)}), bf16[8,2,131072]{2,1,0:T(2,128)(2,1)}, u32[]{:S(2)}, u32[]{:S(2)}) %all-to-all-start.3) | async-done | bytes 4194336 | tf_op jit(solution)/shard_map/all_to_all | solution.py:30
  453.4 10.3 reshape.40
  463.7 9.3 copy.97
  506.6 11.2 fusion.10
  517.8 122.0 %add_add_fusion = (bf16[16,128,512]{1,2,0:T(8,128)(2,1)S(1)}, f32[16,128,512]{1,2,0:T(8,128)}) fusion(f32[16,128,512]{1,2,0:T(8,128)} %bitcast.167, f32[18,130,514]{1,2,0:T(8,128)} %fusion.10, f32[]{:T(128)} %bitcast.79, f32[]{:T(128)} %bitcast.78, f32[]{:T(128)} %bitcast.77, f32[]{:T(128)} %bitcast.76, f32[]{:T(128)} %bitcast.75, f32[]{:T(128)} %bitcast.74, ...), kind=kLoop, calls=%fused_computation.148 | loop fusion | flops 114294784 | bytes 123732184 | tf_op jit(solution)/shard_map/add | solution.py:66
  645.8 24.5 %all-gather.6.cloned.1.call-done = f32[8,128,512]{2,1,0:T(8,128)} async-done(((f32[2,128,512]{2,1,0:T(8,128)}), f32[8,128,512]{2,1,0:T(8,128)}) %all-gather.6.cloned.1.call-update) | async-done | bytes 2097168 | tf_op jit(solution)/shard_map/all_gather | solution.py:111
  713.7 22.6 %fusion.1 = f32[2,18,130,514]{2,3,1,0:T(8,128)S(1)} fusion(bf16[2,1,130,512]{2,3,1,0:T(8,128)(2,1)} %collective-permute-done.7, bf16[2,1,130,512]{2,3,1,0:T(8,128)(2,1)S(1)} %collective-permute-done.6, bf16[2,16,1,512]{2,3,1,0:T(8,128)(2,1)} %copy.73, bf16[2,16,1,512]{2,3,1,0:T(8,128)(2,1)} %copy.72, bf16[1,16,128,512]{2,3,1,0:T(8,128)(2,1)S(1)} %multiply_convert_fusion, ...), kind=kLoop, calls=%fused_computation.8 | loop fusion | flops 50515920 | bytes 14414400 | tf_op jit(solution)/shard_map/convert_element_type | solution.py:119
  743.3 196.9 %fusion.84 = bf16[1,16,128,512]{2,3,1,0:T(8,128)(2,1)S(1)} fusion(f32[18,130,514]{1,2,0:T(8,128)} %get-tuple-element.5, f32[]{:T(128)} %bitcast.79, f32[]{:T(128)} %bitcast.78, f32[]{:T(128)} %bitcast.77, f32[]{:T(128)} %bitcast.76, f32[]{:T(128)} %bitcast.75, f32[]{:T(128)} %bitcast.74, f32[]{:T(128)} %bitcast.73, f32[]{:T(128)} %bitcast.72, f32[]{:T(128)} %bitcast.71, ...), kind=kLoop, calls=%fused_computation.161 | loop fusion | flops 115343360 | bytes 228852000 | tf_op jit(solution)/shard_map/stack | solution.py:124
  943.3 97.5 %all_to_all.143 = bf16[2,16,128,512]{2,1,0,3:T(8,128)(2,1)S(1)} all-to-all(bf16[2,16,128,512]{2,1,0,3:T(8,128)(2,1)S(1)} %copy.74), channel_id=1, replica_groups=mesh['gx'=8,'gz'=4] {'gx'}, dimensions={3} | all-to-all | bytes 8388608 | tf_op jit(solution)/shard_map/all_to_all | solution.py:29
  1061.3 12.9 copy.77
  1074.2 10.5 reshape.41
  1084.7 97.9 %all_to_all.144 = bf16[8,2,131072]{2,1,0:T(2,128)(2,1)} all-to-all(bf16[8,2,131072]{2,1,0:T(2,128)(2,1)} %reshape.41), channel_id=1, replica_groups=mesh['gx'=8,'gz'=4] {'gx'}, dimensions={0} | all-to-all | bytes 8388608 | tf_op jit(solution)/shard_map/all_to_all | solution.py:30
  1182.5 10.3 reshape.42
  1192.8 14.8 %copy.101 = bf16[2,16,128,8,64]{2,1,0,4,3:T(8,128)(2,1)} copy(bf16[2,16,128,8,64]{4,1,0,2,3:T(8,128)(2,1)} %bitcast.172) | data formatting | bytes 8388608 | tf_op jit(solution)/shard_map/all_to_all | solution.py:30
  1207.6 54.1 %all_to_all.145 = bf16[2,16,128,512]{2,1,0,3:T(8,128)(2,1)} all-to-all(bf16[2,16,128,512]{2,1,0,3:T(8,128)(2,1)} %bitcast.174), channel_id=1, replica_groups=mesh['gx'=8,'gz'=4] {'gz'}, dimensions={3} | all-to-all | bytes 8388608 | tf_op jit(solution)/shard_map/all_to_all | solution.py:24
  1276.8 50.7 %all_to_all.146 = bf16[2,64,128,128]{3,2,0,1:T(8,128)(2,1)S(1)} all-to-all(bf16[2,64,128,128]{3,2,0,1:T(8,128)(2,1)S(1)} %copy.84), channel_id=1, replica_groups=mesh['gx'=8,'gz'=4] {'gz'}, dimensions={1} | all-to-all | bytes 8388608 | tf_op jit(solution)/shard_map/all_to_all | solution.py:25
  1340.8 10.4 convolution_add_fusion
  (104 shorter events, 208.7 us)
Async XLA Ops:
  7.2 112.5 %copy-start = (bf16[64,64]{1,0:T(8,128)(2,1)S(1)}, bf16[64,64]{1,0:T(8,128)(2,1)}, u32[]{:S(2)}) copy-start(bf16[64,64]{1,0:T(8,128)(2,1)} %param.10) | copy-start | bytes 24580
  40.4 0.8 copy-start.7
  185.3 123.9 %all-to-all-start.2 = ((bf16[2,16,128,512]{2,1,0,3:T(8,128)(2,1)}), bf16[2,16,128,512]{2,1,0,3:T(8,128)(2,1)}, u32[]{:S(2)}, u32[]{:S(2)}) async-start(bf16[2,16,128,512]{2,1,0,3:T(8,128)(2,1)} %bitcast.175), calls=%async_computation.2 | async-start | bytes 8388608 | tf_op jit(solution)/shard_map/all_to_all | solution.py:29
  191.0 132.4 %all-gather.4.cloned.1.call-start = ((), (), s32[]{:S(2)}) async-start(), calls=%async_computation.8 | async-start | bytes 2359296 | tf_op jit(solution)/shard_map/all_gather | solution.py:71
  356.2 4.9 copy-start.11
  356.2 97.2 %all-to-all-start.3 = ((bf16[8,2,131072]{2,1,0:T(2,128)(2,1)}), bf16[8,2,131072]{2,1,0:T(2,128)(2,1)}, u32[]{:S(2)}, u32[]{:S(2)}) async-start(bf16[8,2,131072]{2,1,0:T(2,128)(2,1)} %reshape.39), calls=%async_computation.3 | async-start | bytes 8388608 | tf_op jit(solution)/shard_map/all_to_all | solution.py:30
  360.9 309.3 %all-gather.6.cloned.1.call-start = ((), (), s32[]{:S(2)}) async-start(), calls=%async_computation.9 | async-start | bytes 2621440 | tf_op jit(solution)/shard_map/all_gather | solution.py:111
  485.1 11.4 collective-permute-start.1
  486.4 8.3 collective-permute-start
  498.3 4.3 copy-start.5
  498.3 4.8 copy-start.4
  499.9 6.0 collective-permute-start.2
  501.4 4.6 collective-permute-start.3
  503.1 2.8 copy-start.2
  503.2 3.4 copy-start.3
  642.8 29.3 %copy-start.10 = (f32[2,128,512]{2,1,0:T(8,128)S(1)}, f32[2,128,512]{2,1,0:T(8,128)}, u32[]{:S(2)}) copy-start(f32[2,128,512]{2,1,0:T(8,128)} %param.7) | copy-start | bytes 1572868
  680.0 4.5 copy-start.1
  688.2 8.7 collective-permute-start.4
  695.6 5.8 collective-permute-start.5
  707.5 3.0 collective-permute-start.6
  708.8 4.9 collective-permute-start.7
  743.3 196.9 %copy-start.6 = (bf16[1,16,128,512]{2,3,1,0:T(8,128)(2,1)S(1)}, bf16[1,16,128,512]{2,3,1,0:T(8,128)(2,1)}, u32[]{:S(2)}) copy-start(bf16[1,16,128,512]{2,3,1,0:T(8,128)(2,1)} %get-tuple-element.11) | copy-start | bytes 6291460
  1045.5 7.4 copy-start.12
  1333.5 7.3 copy-start.8
  (1 other events, 0.8 us)
Sparse Core Ops, SparseCore 0:
  193.9 102.6 all-gather.3
  645.9 24.3 all-gather.5
